TPU v7x, 32 devices: a whole 2x2x4 slice. The times are simulated.
32 devices in a mesh: tm: 8 (over y, x, core), batch: 4 (over z).
Axes of the slice: x: 2, y: 2, z: 4, core: 2. Of those that a mesh axis runs over, the one named last changes fastest.
Arguments:
- signal: bfloat16 [4, 1024, 4096], P('batch', 'tm'), may hold values from -7.5 to 7.5
- gate_input: bfloat16 [4, 1024, 4096], P('batch', 'tm'), may hold values from -6 to 6
- bc_forward: bfloat16 [4, 1024, 128], P('batch', 'tm'), may hold values from -6 to 6
- bc_backward: bfloat16 [4, 1024, 128], P('batch', 'tm'), may hold values from -6 to 6
- step_raw: bfloat16 [4, 1024, 128], P('batch', 'tm'), may hold values from -12 to 2
- decay_rate: float32 [2, 64], replicated, may hold values from 0.3 to 1
- conv_weight: float32 [2, 4, 4224], replicated, may hold values from -3 to 3
- conv_bias: float32 [2, 4224], replicated, may hold values from -1.5 to 1.5
- skip_gain: float32 [2, 64], replicated, may hold values from 0.5 to 1.5
- norm_gain: float32 [4096], replicated, may hold values from 0.1 to 1.9
Outputs:
- mixed: bfloat16 [4, 1024, 4096], P(None, 'batch', 'tm')
All inputs are finite; a program needn't handle non-finite values.
Results may differ from a plain program's by a relative error of at most 0.0075.
Values may be sent and summed in bfloat16 or wider, within the bound.
A program may use at most 256 MiB of HBM per device.

v0:
```python
import functools

import jax
import jax.numpy as jnp
from jax import lax
from jax.experimental import pallas as pl
from jax.experimental.pallas import tpu as pltpu
from jax.sharding import PartitionSpec as P

INNER = 4096
HEADDIM = 64
STATE = 64
HEADS = 64
ROWS = 128
PIECE = 128
GROUP = 512
SPAN = GROUP // PIECE
LAG_LOCAL, LAG_ENTER, LAG_LAST, LAG_PASS = 2, 3, 4, 6
RIM = 16
EPSILON = 1e-05
LOG2E = 1.4426950408889634
MASKED = -1e30

F32 = jnp.float32
BF16 = jnp.bfloat16


def dot(a, b, **kwargs):
    return jnp.dot(a, b, preferred_element_type=F32, **kwargs)


def split_bf16(value):
    high = value.astype(BF16)
    low = (value - high.astype(F32)).astype(BF16)
    return jnp.concatenate([high, low], axis=1)


def half_silu(half):
    return half + half * jnp.tanh(half)


def mixer_kernel(
    tm_count,
    batch_count,
    sig_hbm,
    gate_hbm,
    bcf_hbm,
    bcb_hbm,
    step_hbm,
    rate_hbm,
    cw_hbm,
    cb_hbm,
    skip_hbm,
    gain_hbm,
    out_ref,
    sig_ref,
    gate_ref,
    bcf_ref,
    bcb_ref,
    step_ref,
    rate_ref,
    cw_ref,
    cb_ref,
    skip_ref,
    gain_ref,
    hl_sig,
    hr_sig,
    hl_bc,
    hr_bc,
    tot_buf,
    ext,
    ext_bc,
    xs,
    rt,
    roll_a,
    we,
    we_dw,
    extra,
    dec_f,
    dec_b,
    sgate,
    acc,
    spread_ref,
    keep,
    snd,
    pin,
    csnd,
    crecv,
    esnd,
    ein,
    eown,
    yloc,
    outs,
    mid,
    landing,
    inv_snd,
    inv_buf,
    halo_ssem,
    halo_rsem,
    right_ssem,
    right_rsem,
    left_ssem,
    left_rsem,
    tot_ssem,
    tot_rsem,
    pin_ssem,
    pin_rsem,
    chip_ssem,
    chip_rsem,
    ein_ssem,
    ein_rsem,
    out_ssem,
    out_rsem,
    fwd_ssem,
    fwd_rsem,
    inv_ssem,
    inv_rsem,
    load_sem,
):
    T = tm_count
    M = T // 2
    CW = INNER // T
    HG = CW // HEADDIM
    N = INNER // GROUP
    lap = T // SPAN
    per = T // batch_count
    me = lax.axis_index("tm")
    rec = lax.axis_index("batch")
    core = lax.rem(me, 2)
    chip = me // 2
    forward = core == 1
    partner = me + 1 - 2 * core
    dest = me // per
    place = jnp.where(forward, chip, M - 1 - chip)

    def at(tm, batch=None):
        return {"tm": tm, "batch": rec if batch is None else batch}

    small = [(step_hbm, step_ref), (rate_hbm, rate_ref), (bcf_hbm, bcf_ref), (bcb_hbm, bcb_ref),
             (skip_hbm, skip_ref), (cb_hbm, cb_ref), (cw_hbm, cw_ref), (sig_hbm, sig_ref)]
    late = [(gate_hbm, gate_ref), (gain_hbm, gain_ref)]
    loads = [
        pltpu.make_async_copy(src, dst, load_sem.at[k]) for k, (src, dst) in enumerate(small + late)
    ]
    for load in loads:
        load.start()

    barrier = pltpu.get_barrier_semaphore()

    def greet(tm, batch):
        pl.semaphore_signal(
            barrier, inc=1, device_id={"tm": tm, "batch": batch},
            device_id_type=pl.DeviceIdType.MESH,
        )

    own_dest = dest == rec
    for j in range(T):

        @pl.when(j != me)
        def _():
            greet(j, rec)

        @pl.when(jnp.logical_or(j != me, jnp.logical_not(own_dest)))
        def _():
            greet(j, dest)

    for b in range(batch_count):
        for q in range(per):

            @pl.when(jnp.logical_or(b != rec, rec * per + q != me))
            def _():
                greet(rec * per + q, b)

    for b in range(batch_count):

        @pl.when(b != rec)
        def _():
            greet(me, b)


    def remote(src, dst, ssem, rsem, device):
        return pltpu.make_async_remote_copy(
            src_ref=src, dst_ref=dst, send_sem=ssem, recv_sem=rsem,
            device_id=device, device_id_type=pl.DeviceIdType.MESH,
        )

    spot = lax.broadcasted_iota(jnp.int32, (4 * HEADS, GROUP), 1)
    offset = (lax.broadcasted_iota(jnp.int32, (4 * HEADS, GROUP), 0) & (2 * HEADS - 1)) - (
        (spot >> 7) * HG + ((spot >> 6) & 1)
    )

    def head_of(g):
        return lax.rem(g, lap) * SPAN * HG + 2 * (g // lap)

    def lay_out(g, _):
        spread_ref[0, g] = jnp.where(offset == head_of(g), 1.0, 0.0).astype(BF16)
        spread_ref[1, g] = jnp.where(offset == head_of(g) + HEADS, 1.0, 0.0).astype(BF16)
        return 0

    lax.fori_loop(0, N, lay_out, 0)

    for load in loads[: len(small)]:
        load.wait()
    raw = step_ref[...].astype(F32)
    step = jnp.maximum(raw, 0.0) + jnp.log1p(jnp.exp(-jnp.abs(raw)))
    rate = jnp.concatenate([rate_ref[0:1, :], rate_ref[1:2, :]], axis=1)
    log_decay = -step * rate
    row = lax.broadcasted_iota(jnp.int32, (ROWS, ROWS), 0)
    col = lax.broadcasted_iota(jnp.int32, (ROWS, ROWS), 1)
    lower = row >= col
    upper = row <= col
    fwd_lane = col < HEADS
    high = lax.Precision.HIGHEST
    cum = jnp.where(
        fwd_lane,
        dot(lower.astype(F32), log_decay, precision=high),
        dot(upper.astype(F32), log_decay, precision=high),
    )
    total = jnp.where(fwd_lane[0:1], cum[ROWS - 1 : ROWS], cum[0:1])
    tot_buf[me] = jnp.broadcast_to(total, (8, ROWS))

    def tot_copy(j):
        return remote(tot_buf.at[me], tot_buf.at[me], tot_ssem.at[j], tot_rsem.at[me], at(j))

    skip = jnp.concatenate([skip_ref[0:1, :], skip_ref[1:2, :]], axis=1)
    we[0:ROWS] = split_bf16(jnp.exp(total - cum) * step)
    we[ROWS : 2 * ROWS] = split_bf16(jnp.exp(cum))
    we[2 * ROWS :] = split_bf16(
        jnp.concatenate([jnp.exp(total), skip, jnp.zeros((14, 2 * HEADS), F32)], axis=0)
    )
    rt[...] = (LOG2E * (jnp.log(step) - cum)).T
    roll_a[...] = LOG2E * cum
    own_dir = (lax.broadcasted_iota(jnp.int32, (1, 2 * HEADS), 1) < HEADS) == forward
    acc[...] = jnp.zeros_like(acc)

    def spread(g, direction):
        return spread_ref[direction, g]

    def wide(k):
        return pl.ds(pl.multiple_of(k * SPAN * CW, SPAN * CW), SPAN * CW)

    bc_right = remote(
        bcf_hbm.at[pl.ds(ROWS - RIM, RIM)], hl_bc, halo_ssem.at[0], halo_rsem.at[0], at(me + 1)
    )
    bc_left = remote(bcb_hbm.at[pl.ds(0, RIM)], hr_bc, halo_ssem.at[1], halo_rsem.at[1], at(me - 1))

    def sig_right(g):
        return remote(
            sig_hbm.at[pl.ds(ROWS - RIM, RIM), wide(g)], hl_sig.at[:, wide(g)],
            right_ssem.at[g], right_rsem.at[g], at(me + 1),
        )

    def sig_left(g):
        return remote(
            sig_hbm.at[pl.ds(0, RIM), wide(g)], hr_sig.at[:, wide(g)],
            left_ssem.at[g], left_rsem.at[g], at(me - 1),
        )

    pl.semaphore_wait(barrier, (T - 1) + 2 * (T - jnp.where(own_dest, 1, 0)) + batch_count - 1)

    @pl.when(me < T - 1)
    def _():
        bc_right.start()
        sig_right(0).start()

    @pl.when(me > 0)
    def _():
        bc_left.start()
        sig_left(0).start()

    for g in range(1, lap):

        @pl.when(me < T - 1)
        def _():
            sig_right(g).start()

        @pl.when(me > 0)
        def _():
            sig_left(g).start()

    for j in range(T):

        @pl.when(j != me)
        def _():
            tot_copy(j).start()

    @pl.when(me == 0)
    def _():
        hl_sig[...] = jnp.zeros_like(hl_sig)
        hl_bc[...] = jnp.zeros_like(hl_bc)

    @pl.when(me == T - 1)
    def _():
        hr_sig[...] = jnp.zeros_like(hr_sig)
        hr_bc[...] = jnp.zeros_like(hr_bc)

    @pl.when(me > 0)
    def _():
        bc_right.wait_recv()

    @pl.when(me < T - 1)
    def _():
        bc_left.wait_recv()

    def conv(buf, direction, cols):
        half = 0.5 * cb_ref[direction : direction + 1, cols]
        for k in range(4):
            start = 5 + k if direction == 0 else 11 - k
            tap = 0.5 * cw_ref[direction, k : k + 1, cols]
            half = half + tap * buf[start : start + ROWS, :]
        return half_silu(half).astype(BF16)

    bc_cols = slice(INNER, INNER + 2 * STATE)
    ext_bc[0:8] = hl_bc[...].astype(F32)[8:16]
    ext_bc[8 : 8 + ROWS] = bcf_ref[...].astype(F32)
    bc_f = conv(ext_bc, 0, bc_cols)
    ext_bc[8 : 8 + ROWS] = bcb_ref[...].astype(F32)
    ext_bc[8 + ROWS : 16 + ROWS] = hr_bc[...].astype(F32)[0:8]
    bc_b = conv(ext_bc, 1, bc_cols)
    bt_f = bc_f.astype(F32).T[:STATE].astype(BF16)
    bt_b = bc_b.astype(F32).T[:STATE].astype(BF16)
    c_f = bc_f[:, STATE:]
    c_b = bc_b[:, STATE:]
    scores_f = dot(c_f, bt_f)
    scores_b = dot(c_b, bt_b)
    bias_f = jnp.where(lower, 0.0, MASKED)
    bias_b = jnp.where(upper, 0.0, MASKED)

    def pin_copy(g):
        return remote(snd.at[g], pin.at[g], pin_ssem.at[g], pin_rsem.at[g], at(partner))

    def chip_copy(g, target):
        tm = jnp.where(forward, 2 * target + 1, 2 * (M - 1 - target))
        return remote(
            csnd.at[g], crecv.at[place, g], chip_ssem.at[target, g], chip_rsem.at[place, g], at(tm)
        )

    def recv_chip(g, source):
        return remote(
            csnd.at[g], crecv.at[source, g], chip_ssem.at[source, g], chip_rsem.at[source, g], at(partner)
        )

    own_direction = jnp.where(forward, 0, 1)

    def place_of(g, piece):
        start = (lax.rem(g, lap) * SPAN + piece) * CW + (g // lap) * PIECE
        return (
            pl.ds(pl.multiple_of(start, PIECE), PIECE),
            pl.ds(pl.multiple_of(g * GROUP + piece * PIECE, PIECE), PIECE),
        )

    def cols_of(g):
        return pl.ds(pl.multiple_of(g * GROUP, GROUP), GROUP)

    def first(g):
        @pl.when(jnp.logical_and(me > 0, g < lap))
        def _():
            sig_right(g).wait_recv()

        @pl.when(jnp.logical_and(me < T - 1, g < lap))
        def _():
            sig_left(g).wait_recv()

        for piece in range(SPAN):
            cols, inside = place_of(g, piece)
            buf = ext.at[piece]
            buf[0:8] = hl_sig[:, cols].astype(F32)[8:16]
            buf[8 : 8 + ROWS] = sig_ref[:, cols].astype(F32)
            buf[8 + ROWS : 16 + ROWS] = hr_sig[:, cols].astype(F32)[0:8]
            xs[0:ROWS, inside] = conv(buf, 0, cols)
            xs[ROWS : 2 * ROWS, inside] = conv(buf, 1, cols)
        cols = cols_of(g)
        by_f = dot(we[...], spread(g, 0))
        by_b = dot(we[...], spread(g, 1))
        state_f = dot(bt_f, (xs[0:ROWS, cols].astype(F32) * by_f[0:ROWS]).astype(BF16))
        state_b = dot(bt_b, (xs[ROWS : 2 * ROWS, cols].astype(F32) * by_b[0:ROWS]).astype(BF16))
        snd[g] = jnp.where(forward, state_b, state_f).astype(BF16)
        pin_copy(g).start()
        keep[g] = jnp.where(forward, state_f, state_b)
        dec_f[:, cols] = by_f[ROWS : 2 * ROWS]
        dec_b[:, cols] = by_b[ROWS : 2 * ROWS]
        extra[g, 0:1] = jnp.where(forward, by_f[2 * ROWS : 2 * ROWS + 1], by_b[2 * ROWS : 2 * ROWS + 1])
        extra[g, 1:2] = by_f[2 * ROWS + 1 : 2 * ROWS + 2]
        extra[g, 2:3] = by_b[2 * ROWS + 1 : 2 * ROWS + 2]

    def combine(g):
        pin_copy(g).wait_recv()
        csnd[g] = (pin[g].astype(F32) * extra[g, 0:1] + keep[g]).astype(BF16)
        for target in range(1, M):

            @pl.when(place < target)
            def _():
                chip_copy(g, target).start()

    lane = lax.broadcasted_iota(jnp.int32, (ROWS, 2 * HEADDIM), 1)

    def local(g):
        rolled = pltpu.roll(roll_a[...], lax.rem(2 * HEADS - head_of(g), 2 * HEADS), 1)
        skips = extra[g, 1:3]

        def mixing(h):
            a_f = rolled[:, h : h + 1]
            a_b = rolled[:, HEADS + h : HEADS + h + 1]
            r_f = rt[pl.ds(head_of(g) + h, 1), :]
            r_b = rt[pl.ds(HEADS + head_of(g) + h, 1), :]
            mix_f = (scores_f * jnp.exp2((a_f + r_f) + bias_f)).astype(BF16)
            mix_b = (scores_b * jnp.exp2((a_b + r_b) + bias_b)).astype(BF16)
            return jnp.concatenate([mix_f, mix_b], axis=1)

        for piece in range(SPAN):
            cols, inside = place_of(g, piece)
            x_pair = xs[:, inside]
            head = piece * HG
            stacked = jnp.concatenate([mixing(head), mixing(head + 1)], axis=0)
            both = dot(stacked, x_pair)
            out = jnp.where(lane < HEADDIM, both[:ROWS], both[ROWS:])
            part = slice(piece * PIECE, (piece + 1) * PIECE)
            out = out + skips[0:1, part] * x_pair[:ROWS].astype(F32)
            out = out + skips[1:2, part] * x_pair[ROWS:].astype(F32)
            yloc[:, inside] = out
            sgate[:, inside] = half_silu(0.5 * gate_ref[:, cols].astype(F32))

    for j in range(T):

        @pl.when(j != me)
        def _():
            remote(tot_buf.at[j], tot_buf.at[j], tot_ssem.at[j], tot_rsem.at[j], at(partner)).wait_recv()

    rows = [tot_buf[partner][0:1]]
    chips = [tot_buf[2 * q][0:1] + tot_buf[2 * q + 1][0:1] for q in range(M)]
    for source in range(M - 1):
        sum_f = jnp.zeros((1, 2 * HEADS), F32)
        sum_b = jnp.zeros((1, 2 * HEADS), F32)
        for q in range(source + 1, M):
            sum_f = sum_f + jnp.where(q < place, chips[q], 0.0)
            sum_b = sum_b + jnp.where(q < place, chips[M - 1 - q], 0.0)
        rows.append(jnp.where(forward, sum_f, sum_b))
    padding = -len(rows) % 16
    rows = jnp.exp(jnp.concatenate(rows + [jnp.zeros((padding, 2 * HEADS), F32)], axis=0))
    we_dw[...] = split_bf16(jnp.where(own_dir, rows, 0.0))

    def ein_copy(g):
        return remote(esnd.at[g], ein.at[g], ein_ssem.at[g], ein_rsem.at[g], at(partner))

    def enter(g):
        factors = dot(we_dw[...], spread(g, own_direction))
        entering = keep.at[g]
        entering[...] = jnp.zeros((STATE, GROUP), F32)
        for source in range(M - 1):

            @pl.when(source < place)
            def _():
                recv_chip(g, source).wait_recv()
                entering[...] += factors[source + 1 : source + 2] * crecv[source, g].astype(F32)

        value = entering[...]
        esnd[g] = value.astype(BF16)
        ein_copy(g).start()
        eown[g] = (value * factors[0:1] + pin[g].astype(F32)).astype(BF16)

    slot = lax.rem(me, per)

    def out_copy(step, j):
        return remote(
            outs.at[step * T + j], mid.at[step * T + me],
            out_ssem.at[step * T + j], out_rsem.at[step * T + me], at(j),
        )

    def forward_copy(step, i):
        n = step * T + rec * per + lax.rem(i, per)
        return remote(
            mid.at[step * T + i], landing.at[n], fwd_ssem.at[step * T + i], fwd_rsem.at[n],
            at(me, i // per),
        )

    def pass_on(g):
        for piece in range(SPAN):
            step, i = g // lap, lax.rem(g, lap) * SPAN + piece
            n = step * T + i

            @pl.when(i != me)
            def _():
                remote(outs.at[n], mid.at[n], out_ssem.at[n], out_rsem.at[n], at(partner)).wait_recv()

            @pl.when(i // per == rec)
            def _():
                landing[n] = mid[n]

            @pl.when(i // per != rec)
            def _():
                forward_copy(step, i).start()

    for load in loads[len(small) :]:
        load.wait()

    def last(g):
        cols = cols_of(g)
        ein_copy(g).wait_recv()
        own, other = eown[g], ein[g]
        enter_f = jnp.where(forward, own, other)
        enter_b = jnp.where(forward, other, own)
        y = yloc[:, cols] + dec_f[:, cols] * dot(c_f, enter_f) + dec_b[:, cols] * dot(c_b, enter_b)
        gated = y * sgate[:, cols]
        squares = acc[...]
        for piece in range(SPAN):
            step, j = g // lap, lax.rem(g, lap) * SPAN + piece
            part = gated[:, piece * PIECE : (piece + 1) * PIECE]
            squares = squares + part * part
            outs[step * T + j] = part.astype(BF16)

            @pl.when(j == me)
            def _():
                mid[step * T + j] = outs[step * T + j]

            @pl.when(j != me)
            def _():
                out_copy(step, j).start()

        acc[...] = squares

    def turn(t, _):
        for stage, lag in (
            (first, 0), (combine, 1), (local, LAG_LOCAL), (enter, LAG_ENTER), (last, LAG_LAST),
            (pass_on, LAG_PASS),
        ):

            @pl.when(jnp.logical_and(t >= lag, t < N + lag))
            def _():
                stage(t - lag)

        return 0

    lax.fori_loop(0, N + LAG_LAST, turn, 0)
    mean = jnp.sum(acc[...].T, axis=0, keepdims=True) * (1.0 / INNER)
    inv_snd[...] = jnp.broadcast_to(lax.rsqrt(mean + EPSILON), (8, ROWS))

    def inv_copy(j):
        return remote(
            inv_snd, inv_buf.at[rec * per + slot], inv_ssem.at[j], inv_rsem.at[rec * per + slot],
            at(j, dest),
        )

    for j in range(T):
        mine = jnp.logical_and(own_dest, j == me)

        @pl.when(mine)
        def _():
            inv_buf[rec * per + slot] = inv_snd[...]

        @pl.when(jnp.logical_not(mine))
        def _():
            inv_copy(j).start()

    def rest(t, _):
        pass_on(t)
        return 0

    lax.fori_loop(N + LAG_LAST - LAG_PASS, N, rest, 0)

    gain = gain_ref[:, pl.ds(pl.multiple_of(me * CW, CW), CW)]

    for b in range(batch_count):
        for q in range(per):
            n = b * per + q
            mine = jnp.logical_and(b == rec, rec * per + q == me)

            @pl.when(jnp.logical_not(mine))
            def _():
                remote(inv_snd, inv_buf.at[n], inv_ssem.at[0], inv_rsem.at[n], at(partner)).wait_recv()

            scale = jnp.broadcast_to(inv_buf[n][0:1], (ROWS, ROWS)).T
            for step in range(CW // PIECE):
                k = step * T + n

                @pl.when(b != rec)
                def _():
                    remote(
                        mid.at[0], landing.at[k], fwd_ssem.at[0], fwd_rsem.at[k], at(partner)
                    ).wait_recv()

                inside = slice(step * PIECE, (step + 1) * PIECE)
                piece = landing[k].astype(F32) * scale * gain[:, inside]
                out_ref[b, q * ROWS : (q + 1) * ROWS, inside] = piece.astype(BF16)

    @pl.when(me < T - 1)
    def _():
        bc_right.wait_send()
        for g in range(lap):
            sig_right(g).wait_send()

    @pl.when(me > 0)
    def _():
        bc_left.wait_send()
        for g in range(lap):
            sig_left(g).wait_send()

    for j in range(T):

        @pl.when(j != me)
        def _():
            tot_copy(j).wait_send()

        @pl.when(jnp.logical_not(jnp.logical_and(own_dest, j == me)))
        def _():
            inv_copy(j).wait_send()

        for step in range(CW // PIECE):

            @pl.when(j != me)
            def _():
                out_copy(step, j).wait_send()

            @pl.when(j // per != rec)
            def _():
                forward_copy(step, j).wait_send()

    def sent(g, _):
        pin_copy(g).wait_send()
        ein_copy(g).wait_send()
        for target in range(1, M):

            @pl.when(place < target)
            def _():
                chip_copy(g, target).wait_send()

        return 0

    lax.fori_loop(0, N, sent, 0)


def shards(tm_count, batch_count, signal, gate_input, bc_forward, bc_backward, step_raw,
           decay_rate, conv_weight, conv_bias, skip_gain, norm_gain):
    T, M = tm_count, tm_count // 2
    CW = INNER // T
    per = T // batch_count
    N, lap, pieces = INNER // GROUP, T // SPAN, INNER // PIECE
    vmem = pltpu.VMEM
    dma = pltpu.SemaphoreType.DMA
    args = (signal[0], gate_input[0], bc_forward[0], bc_backward[0], step_raw[0],
            decay_rate, conv_weight, conv_bias, skip_gain, norm_gain.reshape(1, INNER))
    scratch = [vmem(a.shape, a.dtype) for a in args] + [
        vmem((RIM, INNER), BF16),
        vmem((RIM, INNER), BF16),
        vmem((RIM, 2 * STATE), BF16),
        vmem((RIM, 2 * STATE), BF16),
        vmem((T, 8, ROWS), F32),
        vmem((SPAN, ROWS + 16, PIECE), F32),
        vmem((ROWS + 16, 2 * STATE), F32),
        vmem((2 * ROWS, INNER), BF16),
        vmem((2 * HEADS, ROWS), F32),
        vmem((ROWS, 2 * HEADS), F32),
        vmem((2 * ROWS + 16, 4 * HEADS), BF16),
        vmem((-(-M // 16) * 16, 4 * HEADS), BF16),
        vmem((N, 8, GROUP), F32),
        vmem((ROWS, INNER), F32),
        vmem((ROWS, INNER), F32),
        vmem((ROWS, INNER), F32),
        vmem((ROWS, PIECE), F32),
        vmem((2, N, 4 * HEADS, GROUP), BF16),
        vmem((N, STATE, GROUP), F32),
        vmem((N, STATE, GROUP), BF16),
        vmem((N, STATE, GROUP), BF16),
        vmem((N, STATE, GROUP), BF16),
        vmem((M, N, STATE, GROUP), BF16),
        vmem((N, STATE, GROUP), BF16),
        vmem((N, STATE, GROUP), BF16),
        vmem((N, STATE, GROUP), BF16),
        vmem((ROWS, INNER), F32),
        vmem((pieces, ROWS, PIECE), BF16),
        vmem((pieces, ROWS, PIECE), BF16),
        vmem((pieces, ROWS, PIECE), BF16),
        vmem((8, ROWS), F32),
        vmem((T, 8, ROWS), F32),
        dma((2,)),
        dma((2,)),
        dma((lap,)),
        dma((lap,)),
        dma((lap,)),
        dma((lap,)),
        dma((T,)),
        dma((T,)),
        dma((N,)),
        dma((N,)),
        dma((M, N)),
        dma((M, N)),
        dma((N,)),
        dma((N,)),
        dma((pieces,)),
        dma((pieces,)),
        dma((pieces,)),
        dma((pieces,)),
        dma((T,)),
        dma((T,)),
        dma((len(args),)),
    ]
    return pl.pallas_call(
        functools.partial(mixer_kernel, T, batch_count),
        out_shape=pltpu.VMEM((batch_count, per * ROWS, CW), BF16),
        in_specs=[pl.BlockSpec(memory_space=pltpu.HBM)] * len(args),
        out_specs=pl.BlockSpec(memory_space=pltpu.VMEM),
        scratch_shapes=scratch,
        compiler_params=pltpu.CompilerParams(
            collective_id=0, has_side_effects=True, vmem_limit_bytes=62 * 2**20
        ),
        cost_estimate=pl.CostEstimate(
            flops=10**9, bytes_accessed=8 * 2**20, transcendentals=4 * 10**6
        ),
    )(*args)


def solution(mesh):
    in_specs = (P("batch", "tm", None),) * 5 + (P(),) * 5
    return jax.shard_map(
        functools.partial(shards, mesh.shape["tm"], mesh.shape["batch"]),
        mesh=mesh, in_specs=in_specs, out_specs=P(None, "batch", "tm"), check_vma=False,
    )
```

profile of v0, /device:TPU:29, one launch (start us, length us, event | category | flops | bytes accessed | tf_op | source)
XLA Modules:
  0.0 56.0 jit_solution(2448942459974241784)
XLA Ops:
  0.0 55.0 %shard_map.100 = bf16[4,256,512]{2,1,0:T(8,128)(2,1)S(1)} custom-call(bf16[128,4096]{1,0:T(8,128)(2,1)} %bitcast.6, bf16[128,4096]{1,0:T(8,128)(2,1)} %bitcast.7, bf16[128,128]{1,0:T(8,128)(2,1)} %bitcast.8, bf16[128,128]{1,0:T(8,128)(2,1)} %bitcast.9, bf16[128,128]{1,0:T(8,128)(2,1)} %bitcast.10, f32[2,64]{1,0:T(2,128)} %rate_hbm.1, f32[2,4,4224]{2,1,0:T(4,128)} %cw_hbm.1, ...), custom_call_target="tpu_custom_call" | custom-call | flops 1000000000 | bytes 8388608 | tf_op jit(solution)/shard_map/pallas_call | solution.py:696
  55.0 1.0 %copy.12 = bf16[4,256,512]{2,1,0:T(8,128)(2,1)} copy(bf16[4,256,512]{2,1,0:T(8,128)(2,1)S(1)} %shard_map.100) | data formatting | bytes 2097152
where the time goes:
time: 56.1 us; the launch traced here: 56 us
  Pallas kernels  55 us (98%)
  local copies, waits for them, and re-layouts  0.97 us (2%)
    pallas_call x1, Pallas kernels, shards(): pl.pallas_call(functools.partial(mixer_kernel, T, batch_count), out_shape...  55 us

commit v1 on v0

--- a/solution.py
+++ b/solution.py
@@ -18,7 +18,6 @@
 LAG_LOCAL, LAG_ENTER, LAG_LAST, LAG_PASS = 2, 3, 4, 6
 RIM = 16
 EPSILON = 1e-05
-LOG2E = 1.4426950408889634
 MASKED = -1e30
 
 F32 = jnp.float32
@@ -30,9 +29,8 @@
 
 
 def split_bf16(value):
-    high = value.astype(BF16)
-    low = (value - high.astype(F32)).astype(BF16)
-    return jnp.concatenate([high, low], axis=1)
+    high = value.astype(BF16).astype(F32)
+    return jnp.concatenate([high, value - high], axis=1).astype(BF16)
 
 
 def half_silu(half):
@@ -74,7 +72,6 @@
     rt,
     roll_a,
     we,
-    we_dw,
     extra,
     dec_f,
     dec_b,
@@ -184,8 +181,8 @@
             device_id=device, device_id_type=pl.DeviceIdType.MESH,
         )
 
-    spot = lax.broadcasted_iota(jnp.int32, (4 * HEADS, GROUP), 1)
-    offset = (lax.broadcasted_iota(jnp.int32, (4 * HEADS, GROUP), 0) & (2 * HEADS - 1)) - (
+    spot = lax.broadcasted_iota(jnp.int32, (2 * HEADS, GROUP), 1)
+    offset = (lax.broadcasted_iota(jnp.int32, (2 * HEADS, GROUP), 0) & (HEADS - 1)) - (
         (spot >> 7) * HG + ((spot >> 6) & 1)
     )
 
@@ -193,8 +190,7 @@
         return lax.rem(g, lap) * SPAN * HG + 2 * (g // lap)
 
     def lay_out(g, _):
-        spread_ref[0, g] = jnp.where(offset == head_of(g), 1.0, 0.0).astype(BF16)
-        spread_ref[1, g] = jnp.where(offset == head_of(g) + HEADS, 1.0, 0.0).astype(BF16)
+        spread_ref[g] = jnp.where(offset == head_of(g), 1.0, 0.0).astype(BF16)
         return 0
 
     lax.fori_loop(0, N, lay_out, 0)
@@ -222,19 +218,17 @@
     def tot_copy(j):
         return remote(tot_buf.at[me], tot_buf.at[me], tot_ssem.at[j], tot_rsem.at[me], at(j))
 
-    skip = jnp.concatenate([skip_ref[0:1, :], skip_ref[1:2, :]], axis=1)
-    we[0:ROWS] = split_bf16(jnp.exp(total - cum) * step)
-    we[ROWS : 2 * ROWS] = split_bf16(jnp.exp(cum))
-    we[2 * ROWS :] = split_bf16(
-        jnp.concatenate([jnp.exp(total), skip, jnp.zeros((14, 2 * HEADS), F32)], axis=0)
-    )
-    rt[...] = (LOG2E * (jnp.log(step) - cum)).T
-    roll_a[...] = LOG2E * cum
-    own_dir = (lax.broadcasted_iota(jnp.int32, (1, 2 * HEADS), 1) < HEADS) == forward
+    at_end, entered = jnp.exp(total - cum) * step, jnp.exp(cum)
+    we[0:ROWS] = split_bf16(at_end[:, :HEADS])
+    we[ROWS : 2 * ROWS] = split_bf16(entered[:, :HEADS])
+    we[2 * ROWS : 3 * ROWS] = split_bf16(at_end[:, HEADS:])
+    we[3 * ROWS : 4 * ROWS] = split_bf16(entered[:, HEADS:])
+    rt[...] = (jnp.log(step) - cum).T
+    roll_a[...] = cum
     acc[...] = jnp.zeros_like(acc)
 
-    def spread(g, direction):
-        return spread_ref[direction, g]
+    def own_heads(value):
+        return jnp.where(forward, value[:, :HEADS], value[:, HEADS:])
 
     def wide(k):
         return pl.ds(pl.multiple_of(k * SPAN * CW, SPAN * CW), SPAN * CW)
@@ -326,6 +320,26 @@
     bias_f = jnp.where(lower, 0.0, MASKED)
     bias_b = jnp.where(upper, 0.0, MASKED)
 
+    for j in range(T):
+
+        @pl.when(j != me)
+        def _():
+            remote(tot_buf.at[j], tot_buf.at[j], tot_ssem.at[j], tot_rsem.at[j], at(partner)).wait_recv()
+
+    rows = [total, tot_buf[partner][0:1]]
+    chips = [tot_buf[2 * q][0:1] + tot_buf[2 * q + 1][0:1] for q in range(M)]
+    for source in range(M - 1):
+        sum_f = jnp.zeros((1, 2 * HEADS), F32)
+        sum_b = jnp.zeros((1, 2 * HEADS), F32)
+        for q in range(source + 1, M):
+            sum_f = sum_f + jnp.where(q < place, chips[q], 0.0)
+            sum_b = sum_b + jnp.where(q < place, chips[M - 1 - q], 0.0)
+        rows.append(jnp.where(forward, sum_f, sum_b))
+    rows = jnp.exp(own_heads(jnp.concatenate(rows, axis=0)))
+    rows = jnp.concatenate([skip_ref[...], rows], axis=0)
+    padding = jnp.zeros((we.shape[0] - 4 * ROWS - rows.shape[0], HEADS), F32)
+    we[4 * ROWS :] = split_bf16(jnp.concatenate([rows, padding], axis=0))
+
     def pin_copy(g):
         return remote(snd.at[g], pin.at[g], pin_ssem.at[g], pin_rsem.at[g], at(partner))
 
@@ -339,8 +353,6 @@
         return remote(
             csnd.at[g], crecv.at[source, g], chip_ssem.at[source, g], chip_rsem.at[source, g], at(partner)
         )
-
-    own_direction = jnp.where(forward, 0, 1)
 
     def place_of(g, piece):
         start = (lax.rem(g, lap) * SPAN + piece) * CW + (g // lap) * PIECE
@@ -370,22 +382,20 @@
             xs[0:ROWS, inside] = conv(buf, 0, cols)
             xs[ROWS : 2 * ROWS, inside] = conv(buf, 1, cols)
         cols = cols_of(g)
-        by_f = dot(we[...], spread(g, 0))
-        by_b = dot(we[...], spread(g, 1))
-        state_f = dot(bt_f, (xs[0:ROWS, cols].astype(F32) * by_f[0:ROWS]).astype(BF16))
-        state_b = dot(bt_b, (xs[ROWS : 2 * ROWS, cols].astype(F32) * by_b[0:ROWS]).astype(BF16))
+        by = dot(we[...], spread_ref[g])
+        x_f, x_b = xs[0:ROWS, cols].astype(F32), xs[ROWS : 2 * ROWS, cols].astype(F32)
+        state_f = dot(bt_f, (x_f * by[0:ROWS]).astype(BF16))
+        state_b = dot(bt_b, (x_b * by[2 * ROWS : 3 * ROWS]).astype(BF16))
         snd[g] = jnp.where(forward, state_b, state_f).astype(BF16)
         pin_copy(g).start()
         keep[g] = jnp.where(forward, state_f, state_b)
-        dec_f[:, cols] = by_f[ROWS : 2 * ROWS]
-        dec_b[:, cols] = by_b[ROWS : 2 * ROWS]
-        extra[g, 0:1] = jnp.where(forward, by_f[2 * ROWS : 2 * ROWS + 1], by_b[2 * ROWS : 2 * ROWS + 1])
-        extra[g, 1:2] = by_f[2 * ROWS + 1 : 2 * ROWS + 2]
-        extra[g, 2:3] = by_b[2 * ROWS + 1 : 2 * ROWS + 2]
+        dec_f[:, cols] = by[ROWS : 2 * ROWS]
+        dec_b[:, cols] = by[3 * ROWS : 4 * ROWS]
+        extra[g] = by[4 * ROWS :]
 
     def combine(g):
         pin_copy(g).wait_recv()
-        csnd[g] = (pin[g].astype(F32) * extra[g, 0:1] + keep[g]).astype(BF16)
+        csnd[g] = (pin[g].astype(F32) * extra[g, 2:3] + keep[g]).astype(BF16)
         for target in range(1, M):
 
             @pl.when(place < target)
@@ -396,15 +406,15 @@
 
     def local(g):
         rolled = pltpu.roll(roll_a[...], lax.rem(2 * HEADS - head_of(g), 2 * HEADS), 1)
-        skips = extra[g, 1:3]
+        skips = extra[g, 0:2]
 
         def mixing(h):
             a_f = rolled[:, h : h + 1]
             a_b = rolled[:, HEADS + h : HEADS + h + 1]
             r_f = rt[pl.ds(head_of(g) + h, 1), :]
             r_b = rt[pl.ds(HEADS + head_of(g) + h, 1), :]
-            mix_f = (scores_f * jnp.exp2((a_f + r_f) + bias_f)).astype(BF16)
-            mix_b = (scores_b * jnp.exp2((a_b + r_b) + bias_b)).astype(BF16)
+            mix_f = (scores_f * jnp.exp((a_f + r_f) + bias_f)).astype(BF16)
+            mix_b = (scores_b * jnp.exp((a_b + r_b) + bias_b)).astype(BF16)
             return jnp.concatenate([mix_f, mix_b], axis=1)
 
         for piece in range(SPAN):
@@ -420,30 +430,11 @@
             yloc[:, inside] = out
             sgate[:, inside] = half_silu(0.5 * gate_ref[:, cols].astype(F32))
 
-    for j in range(T):
-
-        @pl.when(j != me)
-        def _():
-            remote(tot_buf.at[j], tot_buf.at[j], tot_ssem.at[j], tot_rsem.at[j], at(partner)).wait_recv()
-
-    rows = [tot_buf[partner][0:1]]
-    chips = [tot_buf[2 * q][0:1] + tot_buf[2 * q + 1][0:1] for q in range(M)]
-    for source in range(M - 1):
-        sum_f = jnp.zeros((1, 2 * HEADS), F32)
-        sum_b = jnp.zeros((1, 2 * HEADS), F32)
-        for q in range(source + 1, M):
-            sum_f = sum_f + jnp.where(q < place, chips[q], 0.0)
-            sum_b = sum_b + jnp.where(q < place, chips[M - 1 - q], 0.0)
-        rows.append(jnp.where(forward, sum_f, sum_b))
-    padding = -len(rows) % 16
-    rows = jnp.exp(jnp.concatenate(rows + [jnp.zeros((padding, 2 * HEADS), F32)], axis=0))
-    we_dw[...] = split_bf16(jnp.where(own_dir, rows, 0.0))
-
     def ein_copy(g):
         return remote(esnd.at[g], ein.at[g], ein_ssem.at[g], ein_rsem.at[g], at(partner))
 
     def enter(g):
-        factors = dot(we_dw[...], spread(g, own_direction))
+        factors = extra[g, 3 : 3 + M]
         entering = keep.at[g]
         entering[...] = jnp.zeros((STATE, GROUP), F32)
         for source in range(M - 1):
@@ -634,6 +625,7 @@
     CW = INNER // T
     per = T // batch_count
     N, lap, pieces = INNER // GROUP, T // SPAN, INNER // PIECE
+    few = -(-(M + 3) // 16) * 16
     vmem = pltpu.VMEM
     dma = pltpu.SemaphoreType.DMA
     args = (signal[0], gate_input[0], bc_forward[0], bc_backward[0], step_raw[0],
@@ -649,14 +641,13 @@
         vmem((2 * ROWS, INNER), BF16),
         vmem((2 * HEADS, ROWS), F32),
         vmem((ROWS, 2 * HEADS), F32),
-        vmem((2 * ROWS + 16, 4 * HEADS), BF16),
-        vmem((-(-M // 16) * 16, 4 * HEADS), BF16),
-        vmem((N, 8, GROUP), F32),
+        vmem((4 * ROWS + few, 2 * HEADS), BF16),
+        vmem((N, few, GROUP), F32),
         vmem((ROWS, INNER), F32),
         vmem((ROWS, INNER), F32),
         vmem((ROWS, INNER), F32),
         vmem((ROWS, PIECE), F32),
-        vmem((2, N, 4 * HEADS, GROUP), BF16),
+        vmem((N, 2 * HEADS, GROUP), BF16),
         vmem((N, STATE, GROUP), F32),
         vmem((N, STATE, GROUP), BF16),
         vmem((N, STATE, GROUP), BF16),

time: 56.1 us -> 55.8 us (level)
  no operation moved by 1% of the time
where the time goes in v1:
time: 55.8 us; the launch traced here: 55.6 us
  Pallas kernels  54.7 us (98%)
  local copies, waits for them, and re-layouts  0.97 us (2%)
    pallas_call x1, Pallas kernels, shards(): pl.pallas_call(functools.partial(mixer_kernel, T, batch_count), out_shape...  54.7 us

profile of v1, /device:TPU:29, one launch (start us, length us, event | category | flops | bytes accessed | tf_op | source)
XLA Modules:
  0.0 55.6 jit_solution(361599871072705265)
XLA Ops:
  0.0 54.7 %shard_map.100 = bf16[4,256,512]{2,1,0:T(8,128)(2,1)S(1)} custom-call(bf16[128,4096]{1,0:T(8,128)(2,1)} %bitcast.6, bf16[128,4096]{1,0:T(8,128)(2,1)} %bitcast.7, bf16[128,128]{1,0:T(8,128)(2,1)} %bitcast.8, bf16[128,128]{1,0:T(8,128)(2,1)} %bitcast.9, bf16[128,128]{1,0:T(8,128)(2,1)} %bitcast.10, f32[2,64]{1,0:T(2,128)} %rate_hbm.1, f32[2,4,4224]{2,1,0:T(4,128)} %cw_hbm.1, ...), custom_call_target="tpu_custom_call" | custom-call | flops 1000000000 | bytes 8388608 | tf_op jit(solution)/shard_map/pallas_call | solution.py:687
  54.7 1.0 %copy.12 = bf16[4,256,512]{2,1,0:T(8,128)(2,1)} copy(bf16[4,256,512]{2,1,0:T(8,128)(2,1)S(1)} %shard_map.100) | data formatting | bytes 2097152

commit v2 on v1

--- a/solution.py
+++ b/solution.py
@@ -15,7 +15,7 @@
 PIECE = 128
 GROUP = 512
 SPAN = GROUP // PIECE
-LAG_LOCAL, LAG_ENTER, LAG_LAST, LAG_PASS = 2, 3, 4, 6
+LAG_COMBINE, LAG_ENTER, LAG_LOCAL, LAG_LAST, LAG_PASS = 2, 4, 3, 6, 8
 RIM = 16
 EPSILON = 1e-05
 MASKED = -1e30
@@ -195,6 +195,48 @@
 
     lax.fori_loop(0, N, lay_out, 0)
 
+    def wide(k):
+        return pl.ds(pl.multiple_of(k * SPAN * CW, SPAN * CW), SPAN * CW)
+
+    bc_right = remote(
+        bcf_hbm.at[pl.ds(ROWS - RIM, RIM)], hl_bc, halo_ssem.at[0], halo_rsem.at[0], at(me + 1)
+    )
+    bc_left = remote(bcb_hbm.at[pl.ds(0, RIM)], hr_bc, halo_ssem.at[1], halo_rsem.at[1], at(me - 1))
+
+    def sig_right(g):
+        return remote(
+            sig_hbm.at[pl.ds(ROWS - RIM, RIM), wide(g)], hl_sig.at[:, wide(g)],
+            right_ssem.at[g], right_rsem.at[g], at(me + 1),
+        )
+
+    def sig_left(g):
+        return remote(
+            sig_hbm.at[pl.ds(0, RIM), wide(g)], hr_sig.at[:, wide(g)],
+            left_ssem.at[g], left_rsem.at[g], at(me - 1),
+        )
+
+    pl.semaphore_wait(barrier, (T - 1) + 2 * (T - jnp.where(own_dest, 1, 0)) + batch_count - 1)
+
+    @pl.when(me < T - 1)
+    def _():
+        bc_right.start()
+        sig_right(0).start()
+
+    @pl.when(me > 0)
+    def _():
+        bc_left.start()
+        sig_left(0).start()
+
+    for g in range(1, lap):
+
+        @pl.when(me < T - 1)
+        def _():
+            sig_right(g).start()
+
+        @pl.when(me > 0)
+        def _():
+            sig_left(g).start()
+
     for load in loads[: len(small)]:
         load.wait()
     raw = step_ref[...].astype(F32)
@@ -230,48 +272,6 @@
     def own_heads(value):
         return jnp.where(forward, value[:, :HEADS], value[:, HEADS:])
 
-    def wide(k):
-        return pl.ds(pl.multiple_of(k * SPAN * CW, SPAN * CW), SPAN * CW)
-
-    bc_right = remote(
-        bcf_hbm.at[pl.ds(ROWS - RIM, RIM)], hl_bc, halo_ssem.at[0], halo_rsem.at[0], at(me + 1)
-    )
-    bc_left = remote(bcb_hbm.at[pl.ds(0, RIM)], hr_bc, halo_ssem.at[1], halo_rsem.at[1], at(me - 1))
-
-    def sig_right(g):
-        return remote(
-            sig_hbm.at[pl.ds(ROWS - RIM, RIM), wide(g)], hl_sig.at[:, wide(g)],
-            right_ssem.at[g], right_rsem.at[g], at(me + 1),
-        )
-
-    def sig_left(g):
-        return remote(
-            sig_hbm.at[pl.ds(0, RIM), wide(g)], hr_sig.at[:, wide(g)],
-            left_ssem.at[g], left_rsem.at[g], at(me - 1),
-        )
-
-    pl.semaphore_wait(barrier, (T - 1) + 2 * (T - jnp.where(own_dest, 1, 0)) + batch_count - 1)
-
-    @pl.when(me < T - 1)
-    def _():
-        bc_right.start()
-        sig_right(0).start()
-
-    @pl.when(me > 0)
-    def _():
-        bc_left.start()
-        sig_left(0).start()
-
-    for g in range(1, lap):
-
-        @pl.when(me < T - 1)
-        def _():
-            sig_right(g).start()
-
-        @pl.when(me > 0)
-        def _():
-            sig_left(g).start()
-
     for j in range(T):
 
         @pl.when(j != me)
@@ -511,8 +511,8 @@
 
     def turn(t, _):
         for stage, lag in (
-            (first, 0), (combine, 1), (local, LAG_LOCAL), (enter, LAG_ENTER), (last, LAG_LAST),
-            (pass_on, LAG_PASS),
+            (first, 0), (combine, LAG_COMBINE), (enter, LAG_ENTER), (local, LAG_LOCAL),
+            (last, LAG_LAST), (pass_on, LAG_PASS),
         ):
 
             @pl.when(jnp.logical_and(t >= lag, t < N + lag))

time: 55.8 us -> 57.2 us (1.025)
  Pallas kernels: 54.7 us -> 56 us
    pallas_call x1, Pallas kernels: 54.7 us -> 56 us  [shards(): pl.pallas_call(functools.partial(mixer_kernel, T, batch_count), out_shape...]
where the time goes in v2:
time: 57.2 us; the launch traced here: 57 us
  Pallas kernels  56 us (98%)
  local copies, waits for them, and re-layouts  0.97 us (2%)
    pallas_call x1, Pallas kernels, shards(): pl.pallas_call(functools.partial(mixer_kernel, T, batch_count), out_shape...  56 us

profile of v2, /device:TPU:29, one launch (start us, length us, event | category | flops | bytes accessed | tf_op | source)
XLA Modules:
  0.0 57.0 jit_solution(10784236016655641773)
XLA Ops:
  0.0 56.0 %shard_map.100 = bf16[4,256,512]{2,1,0:T(8,128)(2,1)S(1)} custom-call(bf16[128,4096]{1,0:T(8,128)(2,1)} %bitcast.6, bf16[128,4096]{1,0:T(8,128)(2,1)} %bitcast.7, bf16[128,128]{1,0:T(8,128)(2,1)} %bitcast.8, bf16[128,128]{1,0:T(8,128)(2,1)} %bitcast.9, bf16[128,128]{1,0:T(8,128)(2,1)} %bitcast.10, f32[2,64]{1,0:T(2,128)} %rate_hbm.1, f32[2,4,4224]{2,1,0:T(4,128)} %cw_hbm.1, ...), custom_call_target="tpu_custom_call" | custom-call | flops 1000000000 | bytes 8388608 | tf_op jit(solution)/shard_map/pallas_call | solution.py:687
  56.1 1.0 %copy.12 = bf16[4,256,512]{2,1,0:T(8,128)(2,1)} copy(bf16[4,256,512]{2,1,0:T(8,128)(2,1)S(1)} %shard_map.100) | data formatting | bytes 2097152

commit v3 on v2

--- a/solution.py
+++ b/solution.py
@@ -13,9 +13,9 @@
 HEADS = 64
 ROWS = 128
 PIECE = 128
-GROUP = 512
+GROUP = 1024
 SPAN = GROUP // PIECE
-LAG_COMBINE, LAG_ENTER, LAG_LOCAL, LAG_LAST, LAG_PASS = 2, 4, 3, 6, 8
+LAG_COMBINE, LAG_LOCAL, LAG_ENTER, LAG_LAST, LAG_PASS = 1, 2, 3, 4, 5
 RIM = 16
 EPSILON = 1e-05
 MASKED = -1e30
@@ -278,6 +278,24 @@
         def _():
             tot_copy(j).start()
 
+    def place_of(g, piece):
+        start = (lax.rem(g, lap) * SPAN + piece) * CW + (g // lap) * PIECE
+        return (
+            pl.ds(pl.multiple_of(start, PIECE), PIECE),
+            pl.ds(pl.multiple_of(g * GROUP + piece * PIECE, PIECE), PIECE),
+        )
+
+    for load in loads[len(small) :]:
+        load.wait()
+
+    def gate_of(g, _):
+        for piece in range(SPAN):
+            cols, inside = place_of(g, piece)
+            sgate[:, inside] = half_silu(0.5 * gate_ref[:, cols].astype(F32))
+        return 0
+
+    lax.fori_loop(0, N, gate_of, 0)
+
     @pl.when(me == 0)
     def _():
         hl_sig[...] = jnp.zeros_like(hl_sig)
@@ -352,13 +370,6 @@
     def recv_chip(g, source):
         return remote(
             csnd.at[g], crecv.at[source, g], chip_ssem.at[source, g], chip_rsem.at[source, g], at(partner)
-        )
-
-    def place_of(g, piece):
-        start = (lax.rem(g, lap) * SPAN + piece) * CW + (g // lap) * PIECE
-        return (
-            pl.ds(pl.multiple_of(start, PIECE), PIECE),
-            pl.ds(pl.multiple_of(g * GROUP + piece * PIECE, PIECE), PIECE),
         )
 
     def cols_of(g):
@@ -418,7 +429,7 @@
             return jnp.concatenate([mix_f, mix_b], axis=1)
 
         for piece in range(SPAN):
-            cols, inside = place_of(g, piece)
+            _, inside = place_of(g, piece)
             x_pair = xs[:, inside]
             head = piece * HG
             stacked = jnp.concatenate([mixing(head), mixing(head + 1)], axis=0)
@@ -428,7 +439,6 @@
             out = out + skips[0:1, part] * x_pair[:ROWS].astype(F32)
             out = out + skips[1:2, part] * x_pair[ROWS:].astype(F32)
             yloc[:, inside] = out
-            sgate[:, inside] = half_silu(0.5 * gate_ref[:, cols].astype(F32))
 
     def ein_copy(g):
         return remote(esnd.at[g], ein.at[g], ein_ssem.at[g], ein_rsem.at[g], at(partner))
@@ -480,9 +490,6 @@
             @pl.when(i // per != rec)
             def _():
                 forward_copy(step, i).start()
-
-    for load in loads[len(small) :]:
-        load.wait()
 
     def last(g):
         cols = cols_of(g)
@@ -511,7 +518,7 @@
 
     def turn(t, _):
         for stage, lag in (
-            (first, 0), (combine, LAG_COMBINE), (enter, LAG_ENTER), (local, LAG_LOCAL),
+            (first, 0), (combine, LAG_COMBINE), (local, LAG_LOCAL), (enter, LAG_ENTER),
             (last, LAG_LAST), (pass_on, LAG_PASS),
         ):
 

time: 57.2 us -> 57.5 us (level)
  no operation moved by 1% of the time
where the time goes in v3:
time: 57.5 us; the launch traced here: 57.4 us
  Pallas kernels  56.4 us (98%)
  local copies, waits for them, and re-layouts  0.97 us (2%)
    pallas_call x1, Pallas kernels, shards(): pl.pallas_call(functools.partial(mixer_kernel, T, batch_count), out_shape...  56.4 us

profile of v3, /device:TPU:29, one launch (start us, length us, event | category | flops | bytes accessed | tf_op | source)
XLA Modules:
  0.0 57.4 jit_solution(3009667472816027552)
XLA Ops:
  0.0 56.4 %shard_map.100 = bf16[4,256,512]{2,1,0:T(8,128)(2,1)S(1)} custom-call(bf16[128,4096]{1,0:T(8,128)(2,1)} %bitcast.6, bf16[128,4096]{1,0:T(8,128)(2,1)} %bitcast.7, bf16[128,128]{1,0:T(8,128)(2,1)} %bitcast.8, bf16[128,128]{1,0:T(8,128)(2,1)} %bitcast.9, bf16[128,128]{1,0:T(8,128)(2,1)} %bitcast.10, f32[2,64]{1,0:T(2,128)} %rate_hbm.1, f32[2,4,4224]{2,1,0:T(4,128)} %cw_hbm.1, ...), custom_call_target="tpu_custom_call" | custom-call | flops 1000000000 | bytes 8388608 | tf_op jit(solution)/shard_map/pallas_call | solution.py:694
  56.4 1.0 %copy.12 = bf16[4,256,512]{2,1,0:T(8,128)(2,1)} copy(bf16[4,256,512]{2,1,0:T(8,128)(2,1)S(1)} %shard_map.100) | data formatting | bytes 2097152

commit v4 on v3

--- a/solution.py
+++ b/solution.py
@@ -13,9 +13,9 @@
 HEADS = 64
 ROWS = 128
 PIECE = 128
-GROUP = 1024
+GROUP = 512
 SPAN = GROUP // PIECE
-LAG_COMBINE, LAG_LOCAL, LAG_ENTER, LAG_LAST, LAG_PASS = 1, 2, 3, 4, 5
+LAG_COMBINE, LAG_LOCAL, LAG_ENTER, LAG_LAST, LAG_PASS = 1, 2, 3, 4, 6
 RIM = 16
 EPSILON = 1e-05
 MASKED = -1e30

time: 57.5 us -> 55.7 us (0.969)
  Pallas kernels: 56.4 us -> 54.6 us
    pallas_call x1, Pallas kernels: 56.4 us -> 54.6 us  [shards(): pl.pallas_call(functools.partial(mixer_kernel, T, batch_count), out_shape...]
where the time goes in v4:
time: 55.7 us; the launch traced here: 55.6 us
  Pallas kernels  54.6 us (98%)
  local copies, waits for them, and re-layouts  0.97 us (2%)
    pallas_call x1, Pallas kernels, shards(): pl.pallas_call(functools.partial(mixer_kernel, T, batch_count), out_shape...  54.6 us

profile of v4, /device:TPU:29, one launch (start us, length us, event | category | flops | bytes accessed | tf_op | source)
XLA Modules:
  0.0 55.6 jit_solution(3747208520584993055)
XLA Ops:
  0.0 54.6 %shard_map.100 = bf16[4,256,512]{2,1,0:T(8,128)(2,1)S(1)} custom-call(bf16[128,4096]{1,0:T(8,128)(2,1)} %bitcast.6, bf16[128,4096]{1,0:T(8,128)(2,1)} %bitcast.7, bf16[128,128]{1,0:T(8,128)(2,1)} %bitcast.8, bf16[128,128]{1,0:T(8,128)(2,1)} %bitcast.9, bf16[128,128]{1,0:T(8,128)(2,1)} %bitcast.10, f32[2,64]{1,0:T(2,128)} %rate_hbm.1, f32[2,4,4224]{2,1,0:T(4,128)} %cw_hbm.1, ...), custom_call_target="tpu_custom_call" | custom-call | flops 1000000000 | bytes 8388608 | tf_op jit(solution)/shard_map/pallas_call | solution.py:694
  54.6 1.0 %copy.12 = bf16[4,256,512]{2,1,0:T(8,128)(2,1)} copy(bf16[4,256,512]{2,1,0:T(8,128)(2,1)S(1)} %shard_map.100) | data formatting | bytes 2097152

commit v5 on v4

--- a/solution.py
+++ b/solution.py
@@ -15,7 +15,7 @@
 PIECE = 128
 GROUP = 512
 SPAN = GROUP // PIECE
-LAG_COMBINE, LAG_LOCAL, LAG_ENTER, LAG_LAST, LAG_PASS = 1, 2, 3, 4, 6
+LAG_COMBINE, LAG_LOCAL, LAG_ENTER, LAG_LAST, LAG_PASS = 1, 2, 3, 4, 5
 RIM = 16
 EPSILON = 1e-05
 MASKED = -1e30

time: 55.7 us -> 54.8 us (0.984)
  Pallas kernels: 54.6 us -> 53.5 us
    pallas_call x1, Pallas kernels: 54.6 us -> 53.5 us  [shards(): pl.pallas_call(functools.partial(mixer_kernel, T, batch_count), out_shape...]
where the time goes in v5:
time: 54.8 us; the launch traced here: 54.5 us
  Pallas kernels  53.5 us (98%)
  local copies, waits for them, and re-layouts  0.97 us (2%)
    pallas_call x1, Pallas kernels, shards(): pl.pallas_call(functools.partial(mixer_kernel, T, batch_count), out_shape...  53.5 us

profile of v5, /device:TPU:29, one launch (start us, length us, event | category | flops | bytes accessed | tf_op | source)
XLA Modules:
  0.0 54.5 jit_solution(928346050492150086)
XLA Ops:
  0.0 53.5 %shard_map.100 = bf16[4,256,512]{2,1,0:T(8,128)(2,1)S(1)} custom-call(bf16[128,4096]{1,0:T(8,128)(2,1)} %bitcast.6, bf16[128,4096]{1,0:T(8,128)(2,1)} %bitcast.7, bf16[128,128]{1,0:T(8,128)(2,1)} %bitcast.8, bf16[128,128]{1,0:T(8,128)(2,1)} %bitcast.9, bf16[128,128]{1,0:T(8,128)(2,1)} %bitcast.10, f32[2,64]{1,0:T(2,128)} %rate_hbm.1, f32[2,4,4224]{2,1,0:T(4,128)} %cw_hbm.1, ...), custom_call_target="tpu_custom_call" | custom-call | flops 1000000000 | bytes 8388608 | tf_op jit(solution)/shard_map/pallas_call | solution.py:694
  53.5 1.0 %copy.12 = bf16[4,256,512]{2,1,0:T(8,128)(2,1)} copy(bf16[4,256,512]{2,1,0:T(8,128)(2,1)S(1)} %shard_map.100) | data formatting | bytes 2097152
